TPU v7x, 256 devices: a whole 4x4x8 slice. The times are simulated.
256 devices in a mesh: seq: 64 (over z, y, core), head: 4 (over x).
Axes of the slice: x: 4, y: 4, z: 8, core: 2. Of those that a mesh axis runs over, the one named last changes fastest.
Arguments:
- queries: bfloat16 [24576, 4096], P(('seq', 'head')), may hold values from -5 to 5
- keys: bfloat16 [24576, 1024], P(('seq', 'head')), may hold values from -5 to 5
- values: bfloat16 [24576, 1024], P(('seq', 'head')), may hold values from -6 to 6
- out_grad: bfloat16 [24576, 4096], P(('seq', 'head')), may hold values from -6 to 6
- lengths: int32 [32], replicated, may hold values from 1 to 16, 256 in all
Outputs:
- query_grad: bfloat16 [24576, 4096], P(('seq', 'head'))
- key_grad: bfloat16 [24576, 1024], P(('seq', 'head'))
- value_grad: bfloat16 [24576, 1024], P(('seq', 'head'))
Inputs may be any that keep to these rules, and one draw needn't show every extreme that they name: Documents fill the sequence: the lengths sum to 256, and one or more documents have the largest length 16.
All inputs are finite; a program needn't handle non-finite values.
Results may differ from a plain program's by a relative error of at most 0.04.
Values may be sent and summed in bfloat16 or wider, within the bound.
A program may use at most 128 MiB of HBM per device.

v0:
```python
import functools
import math

import jax
import jax.numpy as jnp
from jax import lax
from jax.experimental import pallas as pl
from jax.experimental.pallas import tpu as pltpu
from jax.sharding import PartitionSpec as P

MESH = pl.DeviceIdType.MESH
HD = 128
U = 96
NX = 4
SH = NX * U
REACH = 4
WIN = (REACH + 1) * SH
KVL = 2
GR = 4
QT = 256
TILES = GR * SH // QT
ROWS = 17 * U
NEG = -1e30
SCALE = 1.0 / math.sqrt(HD)
EXP2_SCALE = SCALE * math.log2(math.e)
NT = (((1,), (1,)), ((), ()))
TN = (((0,), (0,)), ((), ()))
F32 = jnp.float32
BF16 = jnp.bfloat16


def kernel(
    n_seq,
    lengths, q_in, k_in, v_in, o_in,
    dq_out, dk_out, dv_out,
    kvw, qb, ob, qst, ost, s_buf, d_buf, p_low, s_low, acc, stage, landed, dq_stage, final,
    local_sem, kv_send, kv_recv, qo_send, qo_recv, ctx_send, ctx_recv, ret_send, ret_recv,
    out_send, out_recv,
):
    s = lax.axis_index("seq")
    x = lax.axis_index("head")
    core = lax.rem(s, 2)
    sibling = s + 1 - 2 * core
    ahead = lax.rem(s + 2, n_seq)
    behind = lax.rem(s + n_seq - 2, n_seq)
    peers = [lax.rem(x + d, NX) for d in range(NX)]

    barrier = pltpu.get_barrier_semaphore()
    for d in range(1, NX):
        pl.semaphore_signal(barrier, inc=1, device_id=(s, peers[d]), device_id_type=MESH)
    for other in (sibling, ahead, behind):
        pl.semaphore_signal(barrier, inc=1, device_id=(other, x), device_id_type=MESH)
    pl.semaphore_wait(barrier, NX + 2)

    def remote(src, dst, send, recv, where):
        return pltpu.make_async_remote_copy(
            src_ref=src, dst_ref=dst, send_sem=send, recv_sem=recv,
            device_id=where, device_id_type=MESH,
        )

    def rows(start, size):
        return pl.ds(pl.multiple_of(start, U), size)

    def lanes(start, size):
        return pl.ds(pl.multiple_of(start, HD), size)

    def kv_copy(h, t, d):
        src = (k_in, v_in)[t].at[:, lanes(peers[d] * KVL * HD + h * HD, HD)]
        dst = kvw.at[h, t, rows(REACH * SH + x * U, U), :]
        if d == 0:
            return pltpu.make_async_copy(src, dst, local_sem.at[h, t])
        i = d - 1
        return remote(src, dst, kv_send.at[h, t, i], kv_recv.at[h, t, i], (s, peers[d]))

    def qo_copy(h, t, d):
        wide = GR * HD
        src = (q_in, o_in)[t].at[:, lanes(peers[d] * KVL * wide + h * wide, wide)]
        dst = (qb, ob)[t].at[h, x]
        if d == 0:
            return pltpu.make_async_copy(src, dst, local_sem.at[h, 2 + t])
        i = d - 1
        return remote(src, dst, qo_send.at[h, t, i], qo_recv.at[h, t, i], (s, peers[d]))

    def shard(rel):
        return rows((REACH + rel) * SH, SH)

    def own_ahead(h):
        return remote(kvw.at[h, :, shard(0), :], kvw.at[h, :, shard(-2), :],
                      ctx_send.at[h, 0], ctx_recv.at[h, 0], (ahead, x))

    def relay_ahead(h):
        return remote(kvw.at[h, :, shard(-2), :], kvw.at[h, :, shard(-4), :],
                      ctx_send.at[h, 1], ctx_recv.at[h, 1], (ahead, x))

    def share_near(h):
        return remote(kvw.at[h, :, shard(-2 * core), :], kvw.at[h, :, shard(-1), :],
                      ctx_send.at[h, 2], ctx_recv.at[h, 2], (sibling, x))

    def share_far(h):
        return remote(kvw.at[h, :, shard(-2 - 2 * core), :], kvw.at[h, :, shard(-3), :],
                      ctx_send.at[h, 3], ctx_recv.at[h, 3], (sibling, x))

    for h in range(KVL):
        for d in (2, 1, 3, 0):
            for t in range(2):
                kv_copy(h, t, d).start()
    for h in range(KVL):
        for d in (2, 1, 3, 0):
            for t in range(2):
                qo_copy(h, t, d).start()

    def wait_in(h, copy):
        for t in range(2):
            copy(h, t, 0).wait()
            for d in range(1, NX):
                copy(h, t, d).wait_recv()

    for h in range(KVL):
        wait_in(h, kv_copy)
        own_ahead(h).start()

        @pl.when(core == 0)
        def _():
            share_near(h).start()

    first_unit = s * NX - REACH * NX
    starts = [jnp.int32(-(1 << 20))] * NX
    bound = jnp.int32(0)
    starts = [jnp.int32(0) - first_unit] * NX
    for doc in range(lengths.shape[0]):
        bound = bound + lengths[doc]
        starts = [
            jnp.where(bound <= s * NX + a, bound - first_unit, starts[a]) for a in range(NX)
        ]

    for h in range(KVL):
        own_ahead(h).wait_recv()
        relay_ahead(h).start()

        @pl.when(core == 0)
        def _():
            share_far(h).start()

        @pl.when(core == 1)
        def _():
            share_near(h).start()

    for h in range(KVL):
        relay_ahead(h).wait_recv()

        @pl.when(core == 1)
        def _():
            share_far(h).start()

    acc[...] = jnp.zeros_like(acc)
    for h in range(KVL):
        wait_in(h, qo_copy)
        for a in range(NX):
            for j in range(GR):
                at = (a * GR + j) * U
                qst[h, at:at + U, :] = qb[h, a, :, j * HD:(j + 1) * HD]
                ost[h, at:at + U, :] = ob[h, a, :, j * HD:(j + 1) * HD]
    for h in range(KVL):
        share_near(h).wait_recv()
        share_far(h).wait_recv()

    lane = lax.broadcasted_iota(jnp.int32, (1, QT), 1)
    row = lax.broadcasted_iota(jnp.int32, (U, QT), 0)

    def tile(i, carry):
        h = i // TILES
        tile_at = lax.rem(i, TILES)
        pair = tile_at // (TILES // 2)
        base = pl.multiple_of((1 + 2 * pair) * U, U)
        cols = tile_at * QT + lane
        unit = cols // (GR * U)
        at = lax.rem(cols, U)
        begin = jnp.zeros((1, QT), jnp.int32)
        for a in range(NX):
            begin = jnp.where(unit == a, starts[a], begin)
        tile_rows = pl.ds(pl.multiple_of(tile_at * QT, QT), QT)
        q_tile = qst[h, tile_rows, :]
        o_tile = ost[h, tile_rows, :]

        def bias(b):
            return jnp.where((begin <= b) & (b <= REACH * NX + unit), 0.0, NEG)

        top = jnp.full((8, QT), -3e38, F32)
        for c in range(ROWS // U):
            b = 1 + 2 * pair + c
            keys = kvw[h, 0, pl.ds(base + c * U, U), :]
            scores = lax.dot_general(keys, q_tile, NT, preferred_element_type=F32)
            if c >= 15:
                ok = (b < REACH * NX + unit) | (row <= at)
                scores = jnp.where(ok, scores, NEG)
            s_buf[c * U:(c + 1) * U, :] = scores
            top = jnp.maximum(top, jnp.max(scores.reshape(U // 8, 8, QT), axis=0) + bias(b))
        top = jnp.max(top, axis=0, keepdims=True)

        total = jnp.zeros((8, QT), F32)
        inner = jnp.zeros((8, QT), F32)
        for c in range(ROWS // U):
            b = 1 + 2 * pair + c
            shift = (bias(b) - top) * EXP2_SCALE
            weights = jnp.exp2(s_buf[c * U:(c + 1) * U, :] * EXP2_SCALE + shift)
            vals = kvw[h, 1, pl.ds(base + c * U, U), :]
            dprobs = lax.dot_general(vals, o_tile, NT, preferred_element_type=F32)
            s_buf[c * U:(c + 1) * U, :] = weights
            d_buf[c * U:(c + 1) * U, :] = dprobs
            total = total + jnp.sum(weights.reshape(U // 8, 8, QT), axis=0)
            inner = inner + jnp.sum((weights * dprobs).reshape(U // 8, 8, QT), axis=0)
        inverse = 1.0 / jnp.sum(total, axis=0, keepdims=True)
        delta = jnp.sum(inner, axis=0, keepdims=True) * inverse

        for c in range(ROWS // U):
            probs = s_buf[c * U:(c + 1) * U, :] * inverse
            dscores = probs * (d_buf[c * U:(c + 1) * U, :] - delta)
            p_low[c * U:(c + 1) * U, :] = probs.astype(BF16)
            s_low[c * U:(c + 1) * U, :] = dscores.astype(BF16)
        window = pl.ds(base, ROWS)
        acc[h, 1, window, :] += jnp.dot(p_low[...], o_tile, preferred_element_type=F32)
        acc[h, 0, window, :] += jnp.dot(s_low[...], q_tile, preferred_element_type=F32)
        dq = lax.dot_general(
            s_low[...], kvw[h, 0, window, :], TN, preferred_element_type=F32
        )
        dq_stage[h, tile_rows, :] = (dq * SCALE).astype(BF16)
        return carry

    lax.fori_loop(0, KVL * TILES, tile, 0)

    wide = GR * HD

    def dq_copy(h, d):
        src = qb.at[h, peers[d]]
        dst = dq_out.at[:, lanes(x * KVL * wide + h * wide, wide)]
        if d == 0:
            return pltpu.make_async_copy(src, dst, local_sem.at[h, 4])
        return remote(src, dst, out_send.at[h, 0, d - 1], out_recv.at[h, 0, d - 1], (s, peers[d]))

    def dkv_copy(h, t, d):
        src = final.at[h, t, rows(peers[d] * U, U), :]
        dst = (dk_out, dv_out)[t].at[:, lanes(x * KVL * HD + h * HD, HD)]
        if d == 0:
            return pltpu.make_async_copy(src, dst, local_sem.at[h, 5 + t])
        i = d - 1
        return remote(
            src, dst, out_send.at[h, 1 + t, i], out_recv.at[h, 1 + t, i], (s, peers[d])
        )

    def ret_copy(h, n):
        where = ((sibling, x), (sibling, x), (behind, x), (behind, x))[n]
        return remote(stage.at[h, n], landed.at[h, n], ret_send.at[h, n], ret_recv.at[h, n], where)

    def put(h, n, rel):
        stage[h, n] = acc[h, :, shard(rel), :].astype(BF16)
        ret_copy(h, n).start()

    def take(h, n, rel):
        ret_copy(h, n).wait_recv()
        acc[h, :, shard(rel), :] += landed[h, n].astype(F32)

    for h in range(KVL):
        put(h, 0, -3)
        put(h, 1, -1)
        for a in range(NX):
            for j in range(GR):
                at = (a * GR + j) * U
                qb[h, a, :, j * HD:(j + 1) * HD] = dq_stage[h, at:at + U, :]
        for d in (2, 1, 3, 0):
            dq_copy(h, d).start()
    for h in range(KVL):
        take(h, 0, -2 - 2 * core)
        put(h, 2, -4)
        take(h, 1, -2 * core)
    for h in range(KVL):
        take(h, 2, -2)
        put(h, 3, -2)
    for h in range(KVL):
        take(h, 3, 0)
        final[h, 0] = (acc[h, 0, shard(0), :] * SCALE).astype(BF16)
        final[h, 1] = acc[h, 1, shard(0), :].astype(BF16)
        for d in (2, 1, 3, 0):
            for t in range(2):
                dkv_copy(h, t, d).start()

    for h in range(KVL):
        for d in range(1, NX):
            for t in range(2):
                kv_copy(h, t, d).wait_send()
                qo_copy(h, t, d).wait_send()
                dkv_copy(h, t, d).wait()
            dq_copy(h, d).wait()
        dq_copy(h, 0).wait()
        for t in range(2):
            dkv_copy(h, t, 0).wait()
        for copy in (own_ahead, relay_ahead, share_near, share_far):
            copy(h).wait_send()
        for n in range(4):
            ret_copy(h, n).wait_send()


def on_device(n_seq, queries, keys, values, out_grad, lengths):
    anywhere = pl.BlockSpec(memory_space=pl.ANY)
    dma = pltpu.SemaphoreType.DMA
    return pl.pallas_call(
        functools.partial(kernel, n_seq),
        out_shape=(
            jax.ShapeDtypeStruct(queries.shape, BF16),
            jax.ShapeDtypeStruct(keys.shape, BF16),
            jax.ShapeDtypeStruct(values.shape, BF16),
        ),
        in_specs=[pl.BlockSpec(memory_space=pltpu.SMEM)] + [anywhere] * 4,
        out_specs=(anywhere,) * 3,
        scratch_shapes=[
            pltpu.VMEM((KVL, 2, WIN, HD), BF16),
            pltpu.VMEM((KVL, NX, U, GR * HD), BF16),
            pltpu.VMEM((KVL, NX, U, GR * HD), BF16),
            pltpu.VMEM((KVL, GR * SH, HD), BF16),
            pltpu.VMEM((KVL, GR * SH, HD), BF16),
            pltpu.VMEM((ROWS, QT), F32),
            pltpu.VMEM((ROWS, QT), F32),
            pltpu.VMEM((ROWS, QT), BF16),
            pltpu.VMEM((ROWS, QT), BF16),
            pltpu.VMEM((KVL, 2, WIN, HD), F32),
            pltpu.VMEM((KVL, 4, 2, SH, HD), BF16),
            pltpu.VMEM((KVL, 4, 2, SH, HD), BF16),
            pltpu.VMEM((KVL, GR * SH, HD), BF16),
            pltpu.VMEM((KVL, 2, SH, HD), BF16),
            dma((KVL, 7)),
            dma((KVL, 2, NX - 1)), dma((KVL, 2, NX - 1)),
            dma((KVL, 2, NX - 1)), dma((KVL, 2, NX - 1)),
            dma((KVL, 4)), dma((KVL, 4)),
            dma((KVL, 4)), dma((KVL, 4)),
            dma((KVL, 3, NX - 1)), dma((KVL, 3, NX - 1)),
        ],
        compiler_params=pltpu.CompilerParams(
            collective_id=0, has_side_effects=True, vmem_limit_bytes=48 * 1024 * 1024
        ),
        name="attention_backward",
    )(lengths, queries, keys, values, out_grad)


def solution(mesh):
    spec = P(("seq", "head"), None)
    return jax.shard_map(
        functools.partial(on_device, mesh.shape["seq"]),
        mesh=mesh,
        in_specs=(spec, spec, spec, spec, P()),
        out_specs=(spec, spec, spec),
        check_vma=False,
    )
```

profile of v0, /device:TPU:1, one launch (start us, length us, event | category | flops | bytes accessed | tf_op | source)
XLA Modules:
  0.0 91.3 jit_solution(4457615014312669679)
XLA Ops:
  0.6 0.0 copy-start
  0.6 1.1 %copy-done = bf16[96,4096]{1,0:T(8,128)(2,1)S(1)} copy-done((bf16[96,4096]{1,0:T(8,128)(2,1)S(1)}, bf16[96,4096]{1,0:T(8,128)(2,1)}, u32[]{:S(2)}) %copy-start) | copy-done | bytes 786456
  1.8 0.0 copy-start.1
  1.8 1.1 %copy-done.1 = bf16[96,4096]{1,0:T(8,128)(2,1)S(1)} copy-done((bf16[96,4096]{1,0:T(8,128)(2,1)S(1)}, bf16[96,4096]{1,0:T(8,128)(2,1)}, u32[]{:S(2)}) %copy-start.1) | copy-done | bytes 786456
  2.9 0.0 copy-start.2
  2.9 0.9 %copy-done.2 = bf16[96,1024]{1,0:T(8,128)(2,1)S(1)} copy-done((bf16[96,1024]{1,0:T(8,128)(2,1)S(1)}, bf16[96,1024]{1,0:T(8,128)(2,1)}, u32[]{:S(2)}) %copy-start.2) | copy-done | bytes 196632
  3.8 0.0 copy-start.3
  3.8 0.9 %copy-done.3 = bf16[96,1024]{1,0:T(8,128)(2,1)S(1)} copy-done((bf16[96,1024]{1,0:T(8,128)(2,1)S(1)}, bf16[96,1024]{1,0:T(8,128)(2,1)}, u32[]{:S(2)}) %copy-start.3) | copy-done | bytes 196632
  4.8 0.0 copy-start.4
  4.8 0.7 copy-done.4
  5.4 83.6 %attention_backward.1 = (bf16[96,4096]{1,0:T(8,128)(2,1)S(1)}, bf16[96,1024]{1,0:T(8,128)(2,1)S(1)}, bf16[96,1024]{1,0:T(8,128)(2,1)S(1)}) custom-call(s32[32]{0:T(128)S(1)} %copy-done.4, bf16[96,4096]{1,0:T(8,128)(2,1)S(1)} %copy-done, bf16[96,1024]{1,0:T(8,128)(2,1)S(1)} %copy-done.2, bf16[96,1024]{1,0:T(8,128)(2,1)S(1)} %copy-done.3, ...), custom_call_target="tpu_custom_call" | custom-call | tf_op jit(solution)/shard_map/attention_backward/pallas_call | solution.py:305
  89.1 0.9 copy.11
  89.9 0.7 copy.12
  90.6 0.7 copy.13
Async XLA Ops:
  0.6 1.1 %copy-start = (bf16[96,4096]{1,0:T(8,128)(2,1)S(1)}, bf16[96,4096]{1,0:T(8,128)(2,1)}, u32[]{:S(2)}) copy-start(bf16[96,4096]{1,0:T(8,128)(2,1)} %q_in.1) | copy-start | bytes 2359300
  1.8 1.1 %copy-start.1 = (bf16[96,4096]{1,0:T(8,128)(2,1)S(1)}, bf16[96,4096]{1,0:T(8,128)(2,1)}, u32[]{:S(2)}) copy-start(bf16[96,4096]{1,0:T(8,128)(2,1)} %o_in.1) | copy-start | bytes 2359300
  2.9 0.9 %copy-start.2 = (bf16[96,1024]{1,0:T(8,128)(2,1)S(1)}, bf16[96,1024]{1,0:T(8,128)(2,1)}, u32[]{:S(2)}) copy-start(bf16[96,1024]{1,0:T(8,128)(2,1)} %k_in.1) | copy-start | bytes 589828
  3.8 0.9 %copy-start.3 = (bf16[96,1024]{1,0:T(8,128)(2,1)S(1)}, bf16[96,1024]{1,0:T(8,128)(2,1)}, u32[]{:S(2)}) copy-start(bf16[96,1024]{1,0:T(8,128)(2,1)} %v_in.1) | copy-start | bytes 589828
  4.8 0.7 copy-start.4
where the time goes:
time: 91.5 us; the launch traced here: 91.3 us
  Pallas kernels  83.6 us (91%)
  local copies, waits for them, and re-layouts  7 us (8%)
    pallas_call x1, Pallas kernels, on_device(): pl.pallas_call(functools.partial(kernel, n_seq), out_shape=(jax.ShapeDtyp...  83.6 us
    unnamed x13, local copies, waits for them, and re-layouts  7 us

commit v1 on v0

--- a/solution.py
+++ b/solution.py
@@ -20,6 +20,7 @@
 QT = 256
 TILES = GR * SH // QT
 ROWS = 17 * U
+COLS = GR * SH
 NEG = -1e30
 SCALE = 1.0 / math.sqrt(HD)
 EXP2_SCALE = SCALE * math.log2(math.e)
@@ -33,7 +34,7 @@
     n_seq,
     lengths, q_in, k_in, v_in, o_in,
     dq_out, dk_out, dv_out,
-    kvw, qb, ob, qst, ost, s_buf, d_buf, p_low, s_low, acc, stage, landed, dq_stage, final,
+    kvw, qb, ob, qst, ost, s_buf, d_buf, p_all, s_all, acc, stage, landed, dq_stage, final,
     local_sem, kv_send, kv_recv, qo_send, qo_recv, ctx_send, ctx_recv, ret_send, ret_recv,
     out_send, out_recv,
 ):
@@ -43,14 +44,16 @@
     sibling = s + 1 - 2 * core
     ahead = lax.rem(s + 2, n_seq)
     behind = lax.rem(s + n_seq - 2, n_seq)
+    ahead_far = lax.rem(s + 4, n_seq)
+    behind_far = lax.rem(s + n_seq - 4, n_seq)
     peers = [lax.rem(x + d, NX) for d in range(NX)]
 
     barrier = pltpu.get_barrier_semaphore()
     for d in range(1, NX):
         pl.semaphore_signal(barrier, inc=1, device_id=(s, peers[d]), device_id_type=MESH)
-    for other in (sibling, ahead, behind):
+    for other in (sibling, ahead, behind, ahead_far, behind_far):
         pl.semaphore_signal(barrier, inc=1, device_id=(other, x), device_id_type=MESH)
-    pl.semaphore_wait(barrier, NX + 2)
+    pl.semaphore_wait(barrier, NX + 4)
 
     def remote(src, dst, send, recv, where):
         return pltpu.make_async_remote_copy(
@@ -88,9 +91,9 @@
         return remote(kvw.at[h, :, shard(0), :], kvw.at[h, :, shard(-2), :],
                       ctx_send.at[h, 0], ctx_recv.at[h, 0], (ahead, x))
 
-    def relay_ahead(h):
-        return remote(kvw.at[h, :, shard(-2), :], kvw.at[h, :, shard(-4), :],
-                      ctx_send.at[h, 1], ctx_recv.at[h, 1], (ahead, x))
+    def own_far_ahead(h):
+        return remote(kvw.at[h, :, shard(0), :], kvw.at[h, :, shard(-4), :],
+                      ctx_send.at[h, 1], ctx_recv.at[h, 1], (ahead_far, x))
 
     def share_near(h):
         return remote(kvw.at[h, :, shard(-2 * core), :], kvw.at[h, :, shard(-1), :],
@@ -101,13 +104,10 @@
                       ctx_send.at[h, 3], ctx_recv.at[h, 3], (sibling, x))
 
     for h in range(KVL):
-        for d in (2, 1, 3, 0):
-            for t in range(2):
-                kv_copy(h, t, d).start()
-    for h in range(KVL):
-        for d in (2, 1, 3, 0):
-            for t in range(2):
-                qo_copy(h, t, d).start()
+        for copy in (kv_copy, qo_copy):
+            for d in (2, 1, 3, 0):
+                for t in range(2):
+                    copy(h, t, d).start()
 
     def wait_in(h, copy):
         for t in range(2):
@@ -115,13 +115,45 @@
             for d in range(1, NX):
                 copy(h, t, d).wait_recv()
 
-    for h in range(KVL):
+    def context_send(h):
         wait_in(h, kv_copy)
+
+        @pl.when(core == 0)
+        def _():
+            share_near(h).start()
+
         own_ahead(h).start()
+        own_far_ahead(h).start()
+
+    def context_share_near(h):
+        own_ahead(h).wait_recv()
 
         @pl.when(core == 0)
         def _():
+            share_far(h).start()
+
+        @pl.when(core == 1)
+        def _():
             share_near(h).start()
+
+    def context_share_far(h):
+        own_far_ahead(h).wait_recv()
+
+        @pl.when(core == 1)
+        def _():
+            share_far(h).start()
+
+    def prepare(h):
+        wait_in(h, qo_copy)
+        for a in range(NX):
+            for j in range(GR):
+                at = (a * GR + j) * U
+                qst[h, at:at + U, :] = qb[h, a, :, j * HD:(j + 1) * HD]
+                ost[h, at:at + U, :] = ob[h, a, :, j * HD:(j + 1) * HD]
+        share_near(h).wait_recv()
+        share_far(h).wait_recv()
+
+    context_send(0)
 
     first_unit = s * NX - REACH * NX
     starts = [jnp.int32(-(1 << 20))] * NX
@@ -133,43 +165,15 @@
             jnp.where(bound <= s * NX + a, bound - first_unit, starts[a]) for a in range(NX)
         ]
 
-    for h in range(KVL):
-        own_ahead(h).wait_recv()
-        relay_ahead(h).start()
-
-        @pl.when(core == 0)
-        def _():
-            share_far(h).start()
-
-        @pl.when(core == 1)
-        def _():
-            share_near(h).start()
-
-    for h in range(KVL):
-        relay_ahead(h).wait_recv()
-
-        @pl.when(core == 1)
-        def _():
-            share_far(h).start()
-
-    acc[...] = jnp.zeros_like(acc)
-    for h in range(KVL):
-        wait_in(h, qo_copy)
-        for a in range(NX):
-            for j in range(GR):
-                at = (a * GR + j) * U
-                qst[h, at:at + U, :] = qb[h, a, :, j * HD:(j + 1) * HD]
-                ost[h, at:at + U, :] = ob[h, a, :, j * HD:(j + 1) * HD]
-    for h in range(KVL):
-        share_near(h).wait_recv()
-        share_far(h).wait_recv()
+    for ref in (p_all, s_all):
+        ref[0:U, :] = jnp.zeros((U, COLS), BF16)
+        ref[U:3 * U, COLS // 2:] = jnp.zeros((2 * U, COLS // 2), BF16)
+        ref[18 * U:, :COLS // 2] = jnp.zeros((2 * U, COLS // 2), BF16)
 
     lane = lax.broadcasted_iota(jnp.int32, (1, QT), 1)
     row = lax.broadcasted_iota(jnp.int32, (U, QT), 0)
 
-    def tile(i, carry):
-        h = i // TILES
-        tile_at = lax.rem(i, TILES)
+    def tile(h, tile_at):
         pair = tile_at // (TILES // 2)
         base = pl.multiple_of((1 + 2 * pair) * U, U)
         cols = tile_at * QT + lane
@@ -178,9 +182,9 @@
         begin = jnp.zeros((1, QT), jnp.int32)
         for a in range(NX):
             begin = jnp.where(unit == a, starts[a], begin)
-        tile_rows = pl.ds(pl.multiple_of(tile_at * QT, QT), QT)
-        q_tile = qst[h, tile_rows, :]
-        o_tile = ost[h, tile_rows, :]
+        tile_cols = pl.ds(pl.multiple_of(tile_at * QT, QT), QT)
+        q_tile = qst[h, tile_cols, :]
+        o_tile = ost[h, tile_cols, :]
 
         def bias(b):
             return jnp.where((begin <= b) & (b <= REACH * NX + unit), 0.0, NEG)
@@ -215,18 +219,14 @@
         for c in range(ROWS // U):
             probs = s_buf[c * U:(c + 1) * U, :] * inverse
             dscores = probs * (d_buf[c * U:(c + 1) * U, :] - delta)
-            p_low[c * U:(c + 1) * U, :] = probs.astype(BF16)
-            s_low[c * U:(c + 1) * U, :] = dscores.astype(BF16)
+            key_rows = pl.ds(base + c * U, U)
+            p_all[key_rows, tile_cols] = probs.astype(BF16)
+            s_all[key_rows, tile_cols] = dscores.astype(BF16)
         window = pl.ds(base, ROWS)
-        acc[h, 1, window, :] += jnp.dot(p_low[...], o_tile, preferred_element_type=F32)
-        acc[h, 0, window, :] += jnp.dot(s_low[...], q_tile, preferred_element_type=F32)
         dq = lax.dot_general(
-            s_low[...], kvw[h, 0, window, :], TN, preferred_element_type=F32
+            s_all[window, tile_cols], kvw[h, 0, window, :], TN, preferred_element_type=F32
         )
-        dq_stage[h, tile_rows, :] = (dq * SCALE).astype(BF16)
-        return carry
-
-    lax.fori_loop(0, KVL * TILES, tile, 0)
+        dq_stage[h, tile_cols, :] = (dq * SCALE).astype(BF16)
 
     wide = GR * HD
 
@@ -248,7 +248,7 @@
         )
 
     def ret_copy(h, n):
-        where = ((sibling, x), (sibling, x), (behind, x), (behind, x))[n]
+        where = ((sibling, x), (sibling, x), (behind_far, x), (behind, x))[n]
         return remote(stage.at[h, n], landed.at[h, n], ret_send.at[h, n], ret_recv.at[h, n], where)
 
     def put(h, n, rel):
@@ -259,29 +259,85 @@
         ret_copy(h, n).wait_recv()
         acc[h, :, shard(rel), :] += landed[h, n].astype(F32)
 
-    for h in range(KVL):
-        put(h, 0, -3)
-        put(h, 1, -1)
+    def send_dq(h):
         for a in range(NX):
             for j in range(GR):
                 at = (a * GR + j) * U
                 qb[h, a, :, j * HD:(j + 1) * HD] = dq_stage[h, at:at + U, :]
         for d in (2, 1, 3, 0):
             dq_copy(h, d).start()
-    for h in range(KVL):
-        take(h, 0, -2 - 2 * core)
+
+    def key_grads(h, rel):
+        at = (REACH + rel) * SH
+        acc[h, 1, at:at + SH, :] = jnp.dot(
+            p_all[at:at + SH, :], ost[h], preferred_element_type=F32
+        )
+        acc[h, 0, at:at + SH, :] = jnp.dot(
+            s_all[at:at + SH, :], qst[h], preferred_element_type=F32
+        )
+
+    def all_key_grads(h):
+        key_grads(h, -3)
+        put(h, 0, -3)
+        key_grads(h, -4)
+
+        @pl.when(core == 1)
+        def _():
+            take(h, 0, -4)
+
         put(h, 2, -4)
-        take(h, 1, -2 * core)
-    for h in range(KVL):
-        take(h, 2, -2)
+        key_grads(h, -1)
+        put(h, 1, -1)
+        key_grads(h, -2)
+
+        @pl.when(core == 0)
+        def _():
+            take(h, 0, -2)
+
+        @pl.when(core == 1)
+        def _():
+            take(h, 1, -2)
+
         put(h, 3, -2)
-    for h in range(KVL):
+        key_grads(h, 0)
+
+        @pl.when(core == 0)
+        def _():
+            take(h, 1, 0)
+
+    def send_dkv(h):
+        take(h, 2, 0)
         take(h, 3, 0)
-        final[h, 0] = (acc[h, 0, shard(0), :] * SCALE).astype(BF16)
-        final[h, 1] = acc[h, 1, shard(0), :].astype(BF16)
+        final[h, 0] = (acc[h, 0, REACH * SH:, :] * SCALE).astype(BF16)
+        final[h, 1] = acc[h, 1, REACH * SH:, :].astype(BF16)
         for d in (2, 1, 3, 0):
             for t in range(2):
                 dkv_copy(h, t, d).start()
+
+    def tiles(h, hooks):
+        def step(i, carry):
+            for at, hook in hooks.items():
+                pl.when(i == at)(hook)
+            tile(h, i)
+            return carry
+
+        lax.fori_loop(0, TILES, step, 0)
+
+    context_share_near(0)
+    context_share_far(0)
+    prepare(0)
+    tiles(0, {
+        0: lambda: context_send(1),
+        2: lambda: context_share_near(1),
+        3: lambda: context_share_far(1),
+    })
+    send_dq(0)
+    all_key_grads(0)
+    prepare(1)
+    tiles(1, {3: lambda: send_dkv(0)})
+    send_dq(1)
+    all_key_grads(1)
+    send_dkv(1)
 
     for h in range(KVL):
         for d in range(1, NX):
@@ -293,7 +349,7 @@
         dq_copy(h, 0).wait()
         for t in range(2):
             dkv_copy(h, t, 0).wait()
-        for copy in (own_ahead, relay_ahead, share_near, share_far):
+        for copy in (own_ahead, own_far_ahead, share_near, share_far):
             copy(h).wait_send()
         for n in range(4):
             ret_copy(h, n).wait_send()
@@ -319,8 +375,8 @@
             pltpu.VMEM((KVL, GR * SH, HD), BF16),
             pltpu.VMEM((ROWS, QT), F32),
             pltpu.VMEM((ROWS, QT), F32),
-            pltpu.VMEM((ROWS, QT), BF16),
-            pltpu.VMEM((ROWS, QT), BF16),
+            pltpu.VMEM((WIN, COLS), BF16),
+            pltpu.VMEM((WIN, COLS), BF16),
             pltpu.VMEM((KVL, 2, WIN, HD), F32),
             pltpu.VMEM((KVL, 4, 2, SH, HD), BF16),
             pltpu.VMEM((KVL, 4, 2, SH, HD), BF16),
@@ -334,7 +390,7 @@
             dma((KVL, 3, NX - 1)), dma((KVL, 3, NX - 1)),
         ],
         compiler_params=pltpu.CompilerParams(
-            collective_id=0, has_side_effects=True, vmem_limit_bytes=48 * 1024 * 1024
+            collective_id=0, has_side_effects=True, vmem_limit_bytes=60 * 1024 * 1024
         ),
         name="attention_backward",
     )(lengths, queries, keys, values, out_grad)

time: 91.5 us -> 83.8 us (0.916)
  Pallas kernels: 83.6 us -> 79.2 us
  local copies, waits for them, and re-layouts: 7 us -> 3.78 us
    pallas_call x1, Pallas kernels: 83.6 us -> 79.2 us  [on_device(): pl.pallas_call(functools.partial(kernel, n_seq), out_shape=(jax.ShapeDtyp...]
    unnamed x13 -> x7, local copies, waits for them, and re-layouts: 7 us -> 3.78 us
where the time goes in v1:
time: 83.8 us; the launch traced here: 83.7 us
  Pallas kernels  79.2 us (95%)
  local copies, waits for them, and re-layouts  3.78 us (5%)
    pallas_call x1, Pallas kernels, on_device(): pl.pallas_call(functools.partial(kernel, n_seq), out_shape=(jax.ShapeDtyp...  79.2 us
    unnamed x7, local copies, waits for them, and re-layouts  3.78 us

profile of v1, /device:TPU:1, one launch (start us, length us, event | category | flops | bytes accessed | tf_op | source)
XLA Modules:
  0.0 83.7 jit_solution(566783230357931193)
XLA Ops:
  0.6 79.2 %attention_backward.1 = (bf16[96,4096]{1,0:T(8,128)(2,1)}, bf16[96,1024]{1,0:T(8,128)(2,1)}, bf16[96,1024]{1,0:T(8,128)(2,1)}) custom-call(s32[32]{0:T(128)} %lengths.1, bf16[96,4096]{1,0:T(8,128)(2,1)} %q_in.1, bf16[96,1024]{1,0:T(8,128)(2,1)} %k_in.1, bf16[96,1024]{1,0:T(8,128)(2,1)} %v_in.1, bf16[96,4096]{1,0:T(8,128)(2,1)} %o_in.1), custom_call_target="tpu_custom_call" | custom-call | tf_op jit(solution)/shard_map/attention_backward/pallas_call | solution.py:361
  79.9 0.0 copy-start.1
  79.9 2.1 %copy.11 = bf16[96,4096]{1,0:T(8,128)(2,1)} copy(bf16[96,4096]{1,0:T(8,128)(2,1)} %get-tuple-element.6) | data formatting | bytes 1572864
  82.0 0.0 copy-done.1
  82.0 0.0 copy-start
  82.0 0.7 copy.12
  82.7 0.3 copy-done
  83.0 0.7 copy.13
Async XLA Ops:
  79.9 2.1 %copy-start.1 = (bf16[96,1024]{1,0:T(8,128)(2,1)S(1)}, bf16[96,1024]{1,0:T(8,128)(2,1)}, u32[]{:S(2)}) copy-start(bf16[96,1024]{1,0:T(8,128)(2,1)} %get-tuple-element.7) | copy-start | bytes 589828
  82.0 1.0 %copy-start = (bf16[96,1024]{1,0:T(8,128)(2,1)S(1)}, bf16[96,1024]{1,0:T(8,128)(2,1)}, u32[]{:S(2)}) copy-start(bf16[96,1024]{1,0:T(8,128)(2,1)} %get-tuple-element.8) | copy-start | bytes 589828

commit v2 on v1

--- a/solution.py
+++ b/solution.py
@@ -18,6 +18,8 @@
 KVL = 2
 GR = 4
 QT = 256
+STEP = 4
+DEPTH = 256
 TILES = GR * SH // QT
 ROWS = 17 * U
 COLS = GR * SH
@@ -34,7 +36,7 @@
     n_seq,
     lengths, q_in, k_in, v_in, o_in,
     dq_out, dk_out, dv_out,
-    kvw, qb, ob, qst, ost, s_buf, d_buf, p_all, s_all, acc, stage, landed, dq_stage, final,
+    kvw, qb, ob, qst, ost, s_even, d_even, s_odd, d_odd, p_all, s_all, acc, stage, landed, dq_stage, final,
     local_sem, kv_send, kv_recv, qo_send, qo_recv, ctx_send, ctx_recv, ret_send, ret_recv,
     out_send, out_recv,
 ):
@@ -165,68 +167,123 @@
             jnp.where(bound <= s * NX + a, bound - first_unit, starts[a]) for a in range(NX)
         ]
 
-    for ref in (p_all, s_all):
-        ref[0:U, :] = jnp.zeros((U, COLS), BF16)
-        ref[U:3 * U, COLS // 2:] = jnp.zeros((2 * U, COLS // 2), BF16)
-        ref[18 * U:, :COLS // 2] = jnp.zeros((2 * U, COLS // 2), BF16)
-
+    s_all[...] = jnp.zeros_like(s_all)
     lane = lax.broadcasted_iota(jnp.int32, (1, QT), 1)
     row = lax.broadcasted_iota(jnp.int32, (U, QT), 0)
-
-    def tile(h, tile_at):
+    units = ROWS // U
+
+    def fold(array, how):
+        return how(array.reshape(U // 8, 8, QT), axis=0)
+
+    def geometry(tile_at):
         pair = tile_at // (TILES // 2)
-        base = pl.multiple_of((1 + 2 * pair) * U, U)
         cols = tile_at * QT + lane
         unit = cols // (GR * U)
-        at = lax.rem(cols, U)
         begin = jnp.zeros((1, QT), jnp.int32)
         for a in range(NX):
             begin = jnp.where(unit == a, starts[a], begin)
-        tile_cols = pl.ds(pl.multiple_of(tile_at * QT, QT), QT)
-        q_tile = qst[h, tile_cols, :]
-        o_tile = ost[h, tile_cols, :]
-
-        def bias(b):
+        first = 1 + 2 * pair
+
+        def bias(c):
+            b = first + c
             return jnp.where((begin <= b) & (b <= REACH * NX + unit), 0.0, NEG)
 
-        top = jnp.full((8, QT), -3e38, F32)
-        for c in range(ROWS // U):
-            b = 1 + 2 * pair + c
-            keys = kvw[h, 0, pl.ds(base + c * U, U), :]
+        def ok(c):
+            return (first + c < REACH * NX + unit) | (row <= lax.rem(cols, U))
+
+        return (
+            pl.multiple_of(first * U, U),
+            pl.ds(pl.multiple_of(tile_at * QT, QT), QT),
+            bias,
+            ok,
+        )
+
+    def scores_stage(h, tile_at, sb, db):
+        base, cols, bias, ok = geometry(tile_at)
+        out = {"top": jnp.full((8, QT), -3e38, F32)}
+        pieces = []
+
+        def scores_piece(at, count):
+            q_tile = qst[h, cols, :]
+            keys = kvw[h, 0, pl.ds(base + at * U, count * U), :]
             scores = lax.dot_general(keys, q_tile, NT, preferred_element_type=F32)
-            if c >= 15:
-                ok = (b < REACH * NX + unit) | (row <= at)
-                scores = jnp.where(ok, scores, NEG)
-            s_buf[c * U:(c + 1) * U, :] = scores
-            top = jnp.maximum(top, jnp.max(scores.reshape(U // 8, 8, QT), axis=0) + bias(b))
+            for k in range(count):
+                c = at + k
+                part = scores[k * U:(k + 1) * U, :]
+                if c >= units - 2:
+                    part = jnp.where(ok(c), part, NEG)
+                sb[c * U:(c + 1) * U, :] = part
+                out["top"] = jnp.maximum(out["top"], fold(part, jnp.max) + bias(c))
+
+        def dprobs_piece(at, count):
+            vals = kvw[h, 1, pl.ds(base + at * U, count * U), :]
+            db[at * U:(at + count) * U, :] = lax.dot_general(
+                vals, ost[h, cols, :], NT, preferred_element_type=F32
+            )
+
+        for at in range(0, units, STEP):
+            count = min(STEP, units - at)
+            pieces.append(functools.partial(scores_piece, at, count))
+        for at in range(0, units, STEP):
+            count = min(STEP, units - at)
+            pieces.append(functools.partial(dprobs_piece, at, count))
+        return pieces, out
+
+    def exp_stage(tile_at, sb, db, top):
+        _, _, bias, _ = geometry(tile_at)
         top = jnp.max(top, axis=0, keepdims=True)
-
-        total = jnp.zeros((8, QT), F32)
-        inner = jnp.zeros((8, QT), F32)
-        for c in range(ROWS // U):
-            b = 1 + 2 * pair + c
-            shift = (bias(b) - top) * EXP2_SCALE
-            weights = jnp.exp2(s_buf[c * U:(c + 1) * U, :] * EXP2_SCALE + shift)
-            vals = kvw[h, 1, pl.ds(base + c * U, U), :]
-            dprobs = lax.dot_general(vals, o_tile, NT, preferred_element_type=F32)
-            s_buf[c * U:(c + 1) * U, :] = weights
-            d_buf[c * U:(c + 1) * U, :] = dprobs
-            total = total + jnp.sum(weights.reshape(U // 8, 8, QT), axis=0)
-            inner = inner + jnp.sum((weights * dprobs).reshape(U // 8, 8, QT), axis=0)
-        inverse = 1.0 / jnp.sum(total, axis=0, keepdims=True)
-        delta = jnp.sum(inner, axis=0, keepdims=True) * inverse
-
-        for c in range(ROWS // U):
-            probs = s_buf[c * U:(c + 1) * U, :] * inverse
-            dscores = probs * (d_buf[c * U:(c + 1) * U, :] - delta)
+        out = {"total": jnp.zeros((8, QT), F32), "inner": jnp.zeros((8, QT), F32)}
+
+        def piece(c):
+            shift = (bias(c) - top) * EXP2_SCALE
+            weights = jnp.exp2(sb[c * U:(c + 1) * U, :] * EXP2_SCALE + shift)
+            sb[c * U:(c + 1) * U, :] = weights
+            out["total"] = out["total"] + fold(weights, jnp.sum)
+            out["inner"] = out["inner"] + fold(weights * db[c * U:(c + 1) * U, :], jnp.sum)
+
+        return [functools.partial(piece, c) for c in range(units)], out
+
+    def grad_stage(tile_at, sb, db, sums):
+        base, cols, _, _ = geometry(tile_at)
+        inverse = 1.0 / jnp.sum(sums["total"], axis=0, keepdims=True)
+        delta = jnp.sum(sums["inner"], axis=0, keepdims=True) * inverse
+
+        def piece(c):
+            probs = sb[c * U:(c + 1) * U, :] * inverse
+            dscores = probs * (db[c * U:(c + 1) * U, :] - delta)
             key_rows = pl.ds(base + c * U, U)
-            p_all[key_rows, tile_cols] = probs.astype(BF16)
-            s_all[key_rows, tile_cols] = dscores.astype(BF16)
-        window = pl.ds(base, ROWS)
-        dq = lax.dot_general(
-            s_all[window, tile_cols], kvw[h, 0, window, :], TN, preferred_element_type=F32
-        )
-        dq_stage[h, tile_cols, :] = (dq * SCALE).astype(BF16)
+            p_all[key_rows, cols] = probs.astype(BF16)
+            s_all[key_rows, cols] = dscores.astype(BF16)
+
+        return [functools.partial(piece, c) for c in range(units)]
+
+    def query_stage(h, tile_at):
+        base, cols, _, _ = geometry(tile_at)
+        out = {"dq": None}
+
+        def piece(at, size):
+            part = lax.dot_general(
+                s_all[pl.ds(base + at, size), cols],
+                kvw[h, 0, pl.ds(base + at, size), :],
+                TN,
+                preferred_element_type=F32,
+            )
+            out["dq"] = part if out["dq"] is None else out["dq"] + part
+            if at + size == ROWS:
+                dq_stage[h, cols, :] = (out["dq"] * SCALE).astype(BF16)
+
+        return [
+            functools.partial(piece, at, min(DEPTH, ROWS - at)) for at in range(0, ROWS, DEPTH)
+        ]
+
+    def together(*stages):
+        order = [
+            ((n + 0.5) / len(stage), which, piece)
+            for which, stage in enumerate(stages)
+            for n, piece in enumerate(stage)
+        ]
+        for _, _, piece in sorted(order, key=lambda entry: entry[:2]):
+            piece()
 
     wide = GR * HD
 
@@ -268,13 +325,21 @@
             dq_copy(h, d).start()
 
     def key_grads(h, rel):
+        half = COLS // 2
         at = (REACH + rel) * SH
-        acc[h, 1, at:at + SH, :] = jnp.dot(
-            p_all[at:at + SH, :], ost[h], preferred_element_type=F32
-        )
-        acc[h, 0, at:at + SH, :] = jnp.dot(
-            s_all[at:at + SH, :], qst[h], preferred_element_type=F32
-        )
+        parts = [(at, at + SH, 0, COLS)]
+        if rel == -REACH:
+            acc[h, :, 0:U, :] = jnp.zeros((2, U, HD), F32)
+            parts = [(U, 3 * U, 0, half), (3 * U, SH, 0, COLS)]
+        if rel == 0:
+            parts = [(at, at + 2 * U, 0, COLS), (at + 2 * U, at + SH, half, COLS)]
+        for top, end, left, right in parts:
+            acc[h, 1, top:end, :] = jnp.dot(
+                p_all[top:end, left:right], ost[h, left:right, :], preferred_element_type=F32
+            )
+            acc[h, 0, top:end, :] = jnp.dot(
+                s_all[top:end, left:right], qst[h, left:right, :], preferred_element_type=F32
+            )
 
     def all_key_grads(h):
         key_grads(h, -3)
@@ -315,26 +380,38 @@
                 dkv_copy(h, t, d).start()
 
     def tiles(h, hooks):
-        def step(i, carry):
+        even, odd = (s_even, d_even), (s_odd, d_odd)
+        pieces, first = scores_stage(h, 0, *even)
+        together(pieces)
+
+        def step(i, top):
             for at, hook in hooks.items():
                 pl.when(i == at)(hook)
-            tile(h, i)
-            return carry
-
-        lax.fori_loop(0, TILES, step, 0)
+            for now, here, there in ((2 * i, even, odd), (2 * i + 1, odd, even)):
+                before = jnp.maximum(now - 1, 0)
+                after = jnp.minimum(now + 1, TILES - 1)
+                pieces, sums = exp_stage(now, *here, top)
+                together(query_stage(h, before), pieces)
+                following, out = scores_stage(h, after, *there)
+                together(following, grad_stage(now, *here, sums))
+                top = out["top"]
+            return top
+
+        lax.fori_loop(0, TILES // 2, step, first["top"])
+        together(query_stage(h, TILES - 1))
 
     context_share_near(0)
     context_share_far(0)
     prepare(0)
     tiles(0, {
         0: lambda: context_send(1),
-        2: lambda: context_share_near(1),
-        3: lambda: context_share_far(1),
+        1: lambda: context_share_near(1),
+        2: lambda: context_share_far(1),
     })
     send_dq(0)
     all_key_grads(0)
     prepare(1)
-    tiles(1, {3: lambda: send_dkv(0)})
+    tiles(1, {1: lambda: send_dkv(0)})
     send_dq(1)
     all_key_grads(1)
     send_dkv(1)
@@ -373,6 +450,8 @@
             pltpu.VMEM((KVL, NX, U, GR * HD), BF16),
             pltpu.VMEM((KVL, GR * SH, HD), BF16),
             pltpu.VMEM((KVL, GR * SH, HD), BF16),
+            pltpu.VMEM((ROWS, QT), F32),
+            pltpu.VMEM((ROWS, QT), F32),
             pltpu.VMEM((ROWS, QT), F32),
             pltpu.VMEM((ROWS, QT), F32),
             pltpu.VMEM((WIN, COLS), BF16),

time: 83.8 us -> 80.9 us (0.965)
  Pallas kernels: 79.2 us -> 75.8 us
    pallas_call x1, Pallas kernels: 79.2 us -> 75.8 us  [on_device(): pl.pallas_call(functools.partial(kernel, n_seq), out_shape=(jax.ShapeDtyp...]
where the time goes in v2:
time: 80.9 us; the launch traced here: 80.2 us
  Pallas kernels  75.8 us (94%)
  local copies, waits for them, and re-layouts  3.78 us (5%)
    pallas_call x1, Pallas kernels, on_device(): pl.pallas_call(functools.partial(kernel, n_seq), out_shape=(jax.ShapeDtyp...  75.8 us
    unnamed x7, local copies, waits for them, and re-layouts  3.78 us

profile of v2, /device:TPU:1, one launch (start us, length us, event | category | flops | bytes accessed | tf_op | source)
XLA Modules:
  0.0 80.2 jit_solution(5246743193882183791)
XLA Ops:
  0.6 75.8 %attention_backward.1 = (bf16[96,4096]{1,0:T(8,128)(2,1)}, bf16[96,1024]{1,0:T(8,128)(2,1)}, bf16[96,1024]{1,0:T(8,128)(2,1)}) custom-call(s32[32]{0:T(128)} %lengths.1, bf16[96,4096]{1,0:T(8,128)(2,1)} %q_in.1, bf16[96,1024]{1,0:T(8,128)(2,1)} %k_in.1, bf16[96,1024]{1,0:T(8,128)(2,1)} %v_in.1, bf16[96,4096]{1,0:T(8,128)(2,1)} %o_in.1), custom_call_target="tpu_custom_call" | custom-call | tf_op jit(solution)/shard_map/attention_backward/pallas_call | solution.py:438
  76.4 0.0 copy-start.1
  76.4 2.1 %copy.11 = bf16[96,4096]{1,0:T(8,128)(2,1)} copy(bf16[96,4096]{1,0:T(8,128)(2,1)} %get-tuple-element.6) | data formatting | bytes 1572864
  78.5 0.0 copy-done.1
  78.5 0.0 copy-start
  78.5 0.7 copy.12
  79.2 0.3 copy-done
  79.5 0.7 copy.13
Async XLA Ops:
  76.4 2.1 %copy-start.1 = (bf16[96,1024]{1,0:T(8,128)(2,1)S(1)}, bf16[96,1024]{1,0:T(8,128)(2,1)}, u32[]{:S(2)}) copy-start(bf16[96,1024]{1,0:T(8,128)(2,1)} %get-tuple-element.7) | copy-start | bytes 589828
  78.5 1.0 %copy-start = (bf16[96,1024]{1,0:T(8,128)(2,1)S(1)}, bf16[96,1024]{1,0:T(8,128)(2,1)}, u32[]{:S(2)}) copy-start(bf16[96,1024]{1,0:T(8,128)(2,1)} %get-tuple-element.8) | copy-start | bytes 589828

commit v3 on v2

--- a/solution.py
+++ b/solution.py
@@ -19,6 +19,7 @@
 GR = 4
 QT = 256
 STEP = 4
+PARTS = 2
 DEPTH = 256
 TILES = GR * SH // QT
 ROWS = 17 * U
@@ -105,8 +106,8 @@
         return remote(kvw.at[h, :, shard(-2 - 2 * core), :], kvw.at[h, :, shard(-3), :],
                       ctx_send.at[h, 3], ctx_recv.at[h, 3], (sibling, x))
 
-    for h in range(KVL):
-        for copy in (kv_copy, qo_copy):
+    for copy in (kv_copy, qo_copy):
+        for h in range(KVL):
             for d in (2, 1, 3, 0):
                 for t in range(2):
                     copy(h, t, d).start()
@@ -156,6 +157,7 @@
         share_far(h).wait_recv()
 
     context_send(0)
+    context_send(1)
 
     first_unit = s * NX - REACH * NX
     starts = [jnp.int32(-(1 << 20))] * NX
@@ -344,15 +346,15 @@
     def all_key_grads(h):
         key_grads(h, -3)
         put(h, 0, -3)
-        key_grads(h, -4)
-
-        @pl.when(core == 1)
-        def _():
-            take(h, 0, -4)
-
-        put(h, 2, -4)
         key_grads(h, -1)
         put(h, 1, -1)
+        key_grads(h, -4)
+
+        @pl.when(core == 1)
+        def _():
+            take(h, 0, -4)
+
+        put(h, 2, -4)
         key_grads(h, -2)
 
         @pl.when(core == 0)
@@ -404,15 +406,15 @@
     context_share_far(0)
     prepare(0)
     tiles(0, {
-        0: lambda: context_send(1),
         1: lambda: context_share_near(1),
         2: lambda: context_share_far(1),
     })
     send_dq(0)
     all_key_grads(0)
     prepare(1)
-    tiles(1, {1: lambda: send_dkv(0)})
+    tiles(1, {})
     send_dq(1)
+    send_dkv(0)
     all_key_grads(1)
     send_dkv(1)
 
@@ -432,10 +434,30 @@
             ret_copy(h, n).wait_send()
 
 
+def place(dq, dk, dv, dq_out, dk_out, dv_out, dq_held, dk_held, dv_held, sems):
+    held = (dq_held, dk_held, dv_held)
+    moves = []
+    for n in range(PARTS):
+        rows = pl.ds(n * (U // PARTS), U // PARTS)
+        for i, (src, dst) in enumerate(((dq, dq_out), (dk, dk_out), (dv, dv_out))):
+            here = held[i].at[rows, :]
+            moves.append((
+                pltpu.make_async_copy(src.at[rows, :], here, sems.at[0, n, i]),
+                pltpu.make_async_copy(here, dst.at[rows, :], sems.at[1, n, i]),
+            ))
+    for load, _ in moves:
+        load.start()
+    for load, store in moves:
+        load.wait()
+        store.start()
+    for _, store in moves:
+        store.wait()
+
+
 def on_device(n_seq, queries, keys, values, out_grad, lengths):
     anywhere = pl.BlockSpec(memory_space=pl.ANY)
     dma = pltpu.SemaphoreType.DMA
-    return pl.pallas_call(
+    results = pl.pallas_call(
         functools.partial(kernel, n_seq),
         out_shape=(
             jax.ShapeDtypeStruct(queries.shape, BF16),
@@ -473,6 +495,15 @@
         ),
         name="attention_backward",
     )(lengths, queries, keys, values, out_grad)
+    return pl.pallas_call(
+        place,
+        out_shape=tuple(jax.ShapeDtypeStruct(r.shape, r.dtype) for r in results),
+        in_specs=[anywhere] * 3,
+        out_specs=(anywhere,) * 3,
+        scratch_shapes=[pltpu.VMEM(r.shape, r.dtype) for r in results]
+        + [dma((2, PARTS, 3))],
+        name="place_results",
+    )(*results)
 
 
 def solution(mesh):

time: 80.9 us -> 71 us (0.88)
  Pallas kernels: 75.8 us -> 70 us
  local copies, waits for them, and re-layouts: 3.78 us -> 0 us
    pallas_call x1, Pallas kernels: 75.8 us -> 67.9 us  [on_device(): pl.pallas_call(functools.partial(kernel, n_seq), out_shape=(jax.ShapeDtyp...]
    unnamed x7 -> x0, local copies, waits for them, and re-layouts: 3.78 us -> none
    pallas_call x0 -> x1, Pallas kernels: none -> 2.12 us  [on_device(): pl.pallas_call(place, out_shape=tuple((jax.ShapeDtypeStruct(r.shape, r.dt...]
where the time goes in v3:
time: 71 us; the launch traced here: 70.8 us
  Pallas kernels  70 us (99%)
  between operations  0.8 us (1%)
    pallas_call x1, Pallas kernels, on_device(): pl.pallas_call(functools.partial(kernel, n_seq), out_shape=(jax.ShapeDtyp...  67.9 us
    pallas_call x1, Pallas kernels, on_device(): pl.pallas_call(place, out_shape=tuple((jax.ShapeDtypeStruct(r.shape, r.dt...  2.12 us

profile of v3, /device:TPU:1, one launch (start us, length us, event | category | flops | bytes accessed | tf_op | source)
XLA Modules:
  0.0 70.8 jit_solution(15523982023164400740)
XLA Ops:
  0.6 67.9 %attention_backward.1 = (bf16[96,4096]{1,0:T(8,128)(2,1)}, bf16[96,1024]{1,0:T(8,128)(2,1)}, bf16[96,1024]{1,0:T(8,128)(2,1)}) custom-call(s32[32]{0:T(128)} %lengths.1, bf16[96,4096]{1,0:T(8,128)(2,1)} %q_in.1, bf16[96,1024]{1,0:T(8,128)(2,1)} %k_in.1, bf16[96,1024]{1,0:T(8,128)(2,1)} %v_in.1, bf16[96,4096]{1,0:T(8,128)(2,1)} %o_in.1), custom_call_target="tpu_custom_call" | custom-call | tf_op jit(solution)/shard_map/attention_backward/pallas_call | solution.py:460
  68.6 2.1 %place_results.1 = (bf16[96,4096]{1,0:T(8,128)(2,1)}, bf16[96,1024]{1,0:T(8,128)(2,1)}, bf16[96,1024]{1,0:T(8,128)(2,1)}) custom-call(bf16[96,4096]{1,0:T(8,128)(2,1)} %get-tuple-element.6.dq, bf16[96,1024]{1,0:T(8,128)(2,1)} %get-tuple-element.7.dk, bf16[96,1024]{1,0:T(8,128)(2,1)} %get-tuple-element.8.dv), custom_call_target="tpu_custom_call" | custom-call | tf_op jit(solution)/shard_map/place_results/pallas_call | solution.py:498

commit v4 on v3

--- a/solution.py
+++ b/solution.py
@@ -18,7 +18,7 @@
 KVL = 2
 GR = 4
 QT = 256
-STEP = 4
+STEP = 9
 PARTS = 2
 DEPTH = 256
 TILES = GR * SH // QT
@@ -26,7 +26,6 @@
 COLS = GR * SH
 NEG = -1e30
 SCALE = 1.0 / math.sqrt(HD)
-EXP2_SCALE = SCALE * math.log2(math.e)
 NT = (((1,), (1,)), ((), ()))
 TN = (((0,), (0,)), ((), ()))
 F32 = jnp.float32
@@ -37,9 +36,9 @@
     n_seq,
     lengths, q_in, k_in, v_in, o_in,
     dq_out, dk_out, dv_out,
-    kvw, qb, ob, qst, ost, s_even, d_even, s_odd, d_odd, p_all, s_all, acc, stage, landed, dq_stage, final,
+    kvw, qb, ob, qst, ost, s_even, d_even, s_odd, d_odd, p_all, s_all, acc, stage, landed, parts, dq_stage, final,
     local_sem, kv_send, kv_recv, qo_send, qo_recv, ctx_send, ctx_recv, ret_send, ret_recv,
-    out_send, out_recv,
+    out_send, out_recv, part_send, part_recv,
 ):
     s = lax.axis_index("seq")
     x = lax.axis_index("head")
@@ -49,14 +48,18 @@
     behind = lax.rem(s + n_seq - 2, n_seq)
     ahead_far = lax.rem(s + 4, n_seq)
     behind_far = lax.rem(s + n_seq - 4, n_seq)
-    peers = [lax.rem(x + d, NX) for d in range(NX)]
+    peers = [x, x + 1 - 2 * lax.rem(x, 2), lax.rem(x + 2, NX), NX - 1 - x]
+    own_pair = x // 2
+    other_pair = 1 - own_pair
 
     barrier = pltpu.get_barrier_semaphore()
     for d in range(1, NX):
         pl.semaphore_signal(barrier, inc=1, device_id=(s, peers[d]), device_id_type=MESH)
-    for other in (sibling, ahead, behind, ahead_far, behind_far):
-        pl.semaphore_signal(barrier, inc=1, device_id=(other, x), device_id_type=MESH)
-    pl.semaphore_wait(barrier, NX + 4)
+    pl.semaphore_signal(barrier, inc=1, device_id=(sibling, x), device_id_type=MESH)
+    for other in (ahead, behind, ahead_far, behind_far):
+        for d in range(NX):
+            pl.semaphore_signal(barrier, inc=1, device_id=(other, peers[d]), device_id_type=MESH)
+    pl.semaphore_wait(barrier, 5 * NX)
 
     def remote(src, dst, send, recv, where):
         return pltpu.make_async_remote_copy(
@@ -108,7 +111,7 @@
 
     for copy in (kv_copy, qo_copy):
         for h in range(KVL):
-            for d in (2, 1, 3, 0):
+            for d in (2, 3, 1, 0):
                 for t in range(2):
                     copy(h, t, d).start()
 
@@ -146,13 +149,23 @@
         def _():
             share_far(h).start()
 
+    def take_queries(h, pair, dists):
+        for t in range(2):
+            for d in dists:
+                if d == 0:
+                    qo_copy(h, t, d).wait()
+                else:
+                    qo_copy(h, t, d).wait_recv()
+        for k in range(2):
+            a = 2 * pair + k
+            for j in range(GR):
+                at = rows((a * GR + j) * U, U)
+                qst[h, at, :] = qb[h, a, :, j * HD:(j + 1) * HD]
+                ost[h, at, :] = ob[h, a, :, j * HD:(j + 1) * HD]
+
     def prepare(h):
-        wait_in(h, qo_copy)
-        for a in range(NX):
-            for j in range(GR):
-                at = (a * GR + j) * U
-                qst[h, at:at + U, :] = qb[h, a, :, j * HD:(j + 1) * HD]
-                ost[h, at:at + U, :] = ob[h, a, :, j * HD:(j + 1) * HD]
+        take_queries(h, other_pair, (2, 3))
+        take_queries(h, own_pair, (1, 0))
         share_near(h).wait_recv()
         share_far(h).wait_recv()
 
@@ -188,7 +201,10 @@
 
         def bias(c):
             b = first + c
-            return jnp.where((begin <= b) & (b <= REACH * NX + unit), 0.0, NEG)
+            live = begin <= b
+            if c >= units - 2:
+                live = live & (b <= REACH * NX + unit)
+            return jnp.where(live, 0.0, NEG)
 
         def ok(c):
             return (first + c < REACH * NX + unit) | (row <= lax.rem(cols, U))
@@ -216,6 +232,8 @@
                     part = jnp.where(ok(c), part, NEG)
                 sb[c * U:(c + 1) * U, :] = part
                 out["top"] = jnp.maximum(out["top"], fold(part, jnp.max) + bias(c))
+            if at + count == units:
+                out["top"] = jnp.max(out["top"], axis=0, keepdims=True) * SCALE
 
         def dprobs_piece(at, count):
             vals = kvw[h, 1, pl.ds(base + at * U, count * U), :]
@@ -233,12 +251,10 @@
 
     def exp_stage(tile_at, sb, db, top):
         _, _, bias, _ = geometry(tile_at)
-        top = jnp.max(top, axis=0, keepdims=True)
         out = {"total": jnp.zeros((8, QT), F32), "inner": jnp.zeros((8, QT), F32)}
 
         def piece(c):
-            shift = (bias(c) - top) * EXP2_SCALE
-            weights = jnp.exp2(sb[c * U:(c + 1) * U, :] * EXP2_SCALE + shift)
+            weights = jnp.exp(sb[c * U:(c + 1) * U, :] * SCALE + (bias(c) - top))
             sb[c * U:(c + 1) * U, :] = weights
             out["total"] = out["total"] + fold(weights, jnp.sum)
             out["inner"] = out["inner"] + fold(weights * db[c * U:(c + 1) * U, :], jnp.sum)
@@ -296,19 +312,28 @@
             return pltpu.make_async_copy(src, dst, local_sem.at[h, 4])
         return remote(src, dst, out_send.at[h, 0, d - 1], out_recv.at[h, 0, d - 1], (s, peers[d]))
 
-    def dkv_copy(h, t, d):
-        src = final.at[h, t, rows(peers[d] * U, U), :]
-        dst = (dk_out, dv_out)[t].at[:, lanes(x * KVL * HD + h * HD, HD)]
-        if d == 0:
-            return pltpu.make_async_copy(src, dst, local_sem.at[h, 5 + t])
-        i = d - 1
+    def part_copy(h, kind, d):
+        src = stage.at[h, 2 + kind, :, rows(peers[d] * U, U), :]
+        dst = parts.at[h, kind, d]
+        if kind == 2 and d == 0:
+            return pltpu.make_async_copy(src, dst, local_sem.at[h, 5])
+        where = (behind_far, behind, s)[kind]
         return remote(
-            src, dst, out_send.at[h, 1 + t, i], out_recv.at[h, 1 + t, i], (s, peers[d])
+            src, dst, part_send.at[h, kind, d], part_recv.at[h, kind, d], (where, peers[d])
         )
 
+    def result_copy(t):
+        return pltpu.make_async_copy(final.at[t], (dk_out, dv_out)[t], local_sem.at[t, 6])
+
     def ret_copy(h, n):
-        where = ((sibling, x), (sibling, x), (behind_far, x), (behind, x))[n]
-        return remote(stage.at[h, n], landed.at[h, n], ret_send.at[h, n], ret_recv.at[h, n], where)
+        return remote(
+            stage.at[h, n], landed.at[h, n], ret_send.at[h, n], ret_recv.at[h, n], (sibling, x)
+        )
+
+    def put_parts(h, kind, rel):
+        stage[h, 2 + kind] = acc[h, :, shard(rel), :].astype(BF16)
+        for d in (2, 3, 1, 0):
+            part_copy(h, kind, d).start()
 
     def put(h, n, rel):
         stage[h, n] = acc[h, :, shard(rel), :].astype(BF16)
@@ -318,12 +343,13 @@
         ret_copy(h, n).wait_recv()
         acc[h, :, shard(rel), :] += landed[h, n].astype(F32)
 
-    def send_dq(h):
-        for a in range(NX):
+    def send_dq(h, pair, dists):
+        for k in range(2):
+            a = 2 * pair + k
             for j in range(GR):
-                at = (a * GR + j) * U
-                qb[h, a, :, j * HD:(j + 1) * HD] = dq_stage[h, at:at + U, :]
-        for d in (2, 1, 3, 0):
+                at = rows((a * GR + j) * U, U)
+                qb[h, a, :, j * HD:(j + 1) * HD] = dq_stage[h, at, :]
+        for d in dists:
             dq_copy(h, d).start()
 
     def key_grads(h, rel):
@@ -343,43 +369,65 @@
                 s_all[top:end, left:right], qst[h, left:right, :], preferred_element_type=F32
             )
 
-    def all_key_grads(h):
+    def take_far(h):
+        @pl.when(core == 1)
+        def _():
+            take(h, 0, -4)
+
+        put_parts(h, 0, -4)
+
+    def take_near(h):
+        @pl.when(core == 0)
+        def _():
+            take(h, 0, -2)
+
+        @pl.when(core == 1)
+        def _():
+            take(h, 1, -2)
+
+        put_parts(h, 1, -2)
+
+    def take_own(h):
+        @pl.when(core == 0)
+        def _():
+            take(h, 1, 0)
+
+        put_parts(h, 2, 0)
+
+    def take_all(h):
+        take_far(h)
+        take_near(h)
+        take_own(h)
+
+    def all_key_grads(h, last):
         key_grads(h, -3)
         put(h, 0, -3)
         key_grads(h, -1)
         put(h, 1, -1)
         key_grads(h, -4)
-
-        @pl.when(core == 1)
-        def _():
-            take(h, 0, -4)
-
-        put(h, 2, -4)
+        if last:
+            take_far(h)
         key_grads(h, -2)
-
-        @pl.when(core == 0)
-        def _():
-            take(h, 0, -2)
-
-        @pl.when(core == 1)
-        def _():
-            take(h, 1, -2)
-
-        put(h, 3, -2)
+        if last:
+            take_near(h)
         key_grads(h, 0)
-
-        @pl.when(core == 0)
-        def _():
-            take(h, 1, 0)
-
-    def send_dkv(h):
-        take(h, 2, 0)
-        take(h, 3, 0)
-        final[h, 0] = (acc[h, 0, REACH * SH:, :] * SCALE).astype(BF16)
-        final[h, 1] = acc[h, 1, REACH * SH:, :].astype(BF16)
-        for d in (2, 1, 3, 0):
-            for t in range(2):
-                dkv_copy(h, t, d).start()
+        if last:
+            take_own(h)
+
+    def finish(h):
+        for kind in (2, 0, 1):
+            for d in range(NX):
+                if kind == 2 and d == 0:
+                    part_copy(h, kind, d).wait()
+                else:
+                    part_copy(h, kind, d).wait_recv()
+        for d in range(NX):
+            at = lanes(peers[d] * KVL * HD + h * HD, HD)
+            whole = (
+                parts[h, 0, d].astype(F32) + parts[h, 1, d].astype(F32) + parts[h, 2, d].astype(F32)
+            )
+            final[0, :, at] = (whole[0] * SCALE).astype(BF16)
+            final[1, :, at] = whole[1].astype(BF16)
 
     def tiles(h, hooks):
         even, odd = (s_even, d_even), (s_odd, d_odd)
@@ -387,7 +435,7 @@
         together(pieces)
 
         def step(i, top):
-            for at, hook in hooks.items():
+            for at, hook in hooks:
                 pl.when(i == at)(hook)
             for now, here, there in ((2 * i, even, odd), (2 * i + 1, odd, even)):
                 before = jnp.maximum(now - 1, 0)
@@ -405,33 +453,37 @@
     context_share_near(0)
     context_share_far(0)
     prepare(0)
-    tiles(0, {
-        1: lambda: context_share_near(1),
-        2: lambda: context_share_far(1),
-    })
-    send_dq(0)
-    all_key_grads(0)
+    tiles(0, [(1, lambda: context_share_near(1)), (2, lambda: context_share_far(1))])
+    send_dq(0, other_pair, (2, 3))
+    send_dq(0, own_pair, (1, 0))
+    all_key_grads(0, False)
     prepare(1)
-    tiles(1, {})
-    send_dq(1)
-    send_dkv(0)
-    all_key_grads(1)
-    send_dkv(1)
+    tiles(1, [(0, lambda: take_all(0))])
+    send_dq(1, other_pair, (2, 3))
+    send_dq(1, own_pair, (1, 0))
+    all_key_grads(1, True)
+    finish(0)
+    finish(1)
+    for t in range(2):
+        result_copy(t).start()
 
     for h in range(KVL):
         for d in range(1, NX):
             for t in range(2):
                 kv_copy(h, t, d).wait_send()
                 qo_copy(h, t, d).wait_send()
-                dkv_copy(h, t, d).wait()
             dq_copy(h, d).wait()
         dq_copy(h, 0).wait()
-        for t in range(2):
-            dkv_copy(h, t, 0).wait()
         for copy in (own_ahead, own_far_ahead, share_near, share_far):
             copy(h).wait_send()
-        for n in range(4):
+        for n in range(2):
             ret_copy(h, n).wait_send()
+        for kind in range(3):
+            for d in range(NX):
+                if kind < 2 or d > 0:
+                    part_copy(h, kind, d).wait_send()
+    for t in range(2):
+        result_copy(t).wait()
 
 
 def place(dq, dk, dv, dq_out, dk_out, dv_out, dq_held, dk_held, dv_held, sems):
@@ -479,16 +531,18 @@
             pltpu.VMEM((WIN, COLS), BF16),
             pltpu.VMEM((WIN, COLS), BF16),
             pltpu.VMEM((KVL, 2, WIN, HD), F32),
-            pltpu.VMEM((KVL, 4, 2, SH, HD), BF16),
-            pltpu.VMEM((KVL, 4, 2, SH, HD), BF16),
+            pltpu.VMEM((KVL, 5, 2, SH, HD), BF16),
+            pltpu.VMEM((KVL, 2, 2, SH, HD), BF16),
+            pltpu.VMEM((KVL, 3, NX, 2, U, HD), BF16),
             pltpu.VMEM((KVL, GR * SH, HD), BF16),
-            pltpu.VMEM((KVL, 2, SH, HD), BF16),
+            pltpu.VMEM((2, U, NX * KVL * HD), BF16),
             dma((KVL, 7)),
             dma((KVL, 2, NX - 1)), dma((KVL, 2, NX - 1)),
             dma((KVL, 2, NX - 1)), dma((KVL, 2, NX - 1)),
             dma((KVL, 4)), dma((KVL, 4)),
-            dma((KVL, 4)), dma((KVL, 4)),
-            dma((KVL, 3, NX - 1)), dma((KVL, 3, NX - 1)),
+            dma((KVL, 2)), dma((KVL, 2)),
+            dma((KVL, 1, NX - 1)), dma((KVL, 1, NX - 1)),
+            dma((KVL, 3, NX)), dma((KVL, 3, NX)),
         ],
         compiler_params=pltpu.CompilerParams(
             collective_id=0, has_side_effects=True, vmem_limit_bytes=60 * 1024 * 1024

time: 71 us -> 70.9 us (level)
  no operation moved by 1% of the time
where the time goes in v4:
time: 70.9 us; the launch traced here: 70.8 us
  Pallas kernels  70.2 us (99%)
    pallas_call x1, Pallas kernels, on_device(): pl.pallas_call(functools.partial(kernel, n_seq), out_shape=(jax.ShapeDtyp...  68 us
    pallas_call x1, Pallas kernels, on_device(): pl.pallas_call(place, out_shape=tuple((jax.ShapeDtypeStruct(r.shape, r.dt...  2.12 us

profile of v4, /device:TPU:1, one launch (start us, length us, event | category | flops | bytes accessed | tf_op | source)
XLA Modules:
  0.0 70.8 jit_solution(7795168565855857158)
XLA Ops:
  0.6 68.0 %attention_backward.1 = (bf16[96,4096]{1,0:T(8,128)(2,1)}, bf16[96,1024]{1,0:T(8,128)(2,1)}, bf16[96,1024]{1,0:T(8,128)(2,1)}) custom-call(s32[32]{0:T(128)} %lengths.1, bf16[96,4096]{1,0:T(8,128)(2,1)} %q_in.1, bf16[96,1024]{1,0:T(8,128)(2,1)} %k_in.1, bf16[96,1024]{1,0:T(8,128)(2,1)} %v_in.1, bf16[96,4096]{1,0:T(8,128)(2,1)} %o_in.1), custom_call_target="tpu_custom_call" | custom-call | tf_op jit(solution)/shard_map/attention_backward/pallas_call | solution.py:512
  68.7 2.1 %place_results.1 = (bf16[96,4096]{1,0:T(8,128)(2,1)}, bf16[96,1024]{1,0:T(8,128)(2,1)}, bf16[96,1024]{1,0:T(8,128)(2,1)}) custom-call(bf16[96,4096]{1,0:T(8,128)(2,1)} %get-tuple-element.6.dq, bf16[96,1024]{1,0:T(8,128)(2,1)} %get-tuple-element.7.dk, bf16[96,1024]{1,0:T(8,128)(2,1)} %get-tuple-element.8.dv), custom_call_target="tpu_custom_call" | custom-call | tf_op jit(solution)/shard_map/place_results/pallas_call | solution.py:552
